TPU v7x, 128 devices: a whole 4x4x4 slice. The times are simulated.
128 devices in a mesh: row: 8 (over y_lo, z), col: 16 (over x, y_hi, core).
Axes of the slice: x: 4, y: 4 (y_hi: 2, y_lo: 2; y = y_hi * 2 + y_lo), z: 4, core: 2. Of those that a mesh axis runs over, the one named last changes fastest.
Arguments:
- hessian: float32 [16384, 8, 16, 128], P('row', None, 'col'), may hold values from -1 to 16, as said below
- weights: bfloat16 [512, 16384], P('col', 'row'), may hold values from -6 to 6
- codes: int32 [512, 8192], P('col', 'row'), may hold values from 0 to 255
- tile_map: int32 [32, 64], P('col', 'row'), may hold values from 0 to 511
- codebooks: float32 [512, 2, 256], replicated, may hold values from -6 to 6
Outputs:
- adjusted_codebooks: float32 [512, 2, 256], replicated
Inputs may be any that keep to these rules, and one draw needn't show every extreme that they name: `hessian`: H is symmetric with a dominant positive diagonal.
All inputs are finite; a program needn't handle non-finite values.
Results may differ from a plain program's by a relative error of at most 0.0003.
Values sent between devices are 32-bit elements; how exact they have to be, the bound alone decides.
No kernel may reach another device: no remote copies, remote signals or barrier semaphores. Data moves between devices by JAX's collectives and lax.ppermute only.
A program may use at most 64 MiB of HBM per device.

v0:
```python
import jax
import jax.numpy as jnp
from jax import lax
from jax.sharding import PartitionSpec as P

CODES = 256
NB = 512
TILE_ROWS = 16
TILE_COLS = 256
STEPS = 2
learn_rate = 0.01


def per_device(hessian, weights, codes, tile_map, codebooks):
    rows_local, cols_local = weights.shape
    rows_tiles = rows_local // TILE_ROWS
    cols_tiles = cols_local // TILE_COLS
    tile_count = rows_tiles * cols_tiles
    half_width = TILE_COLS // 2
    pair_count = TILE_ROWS * half_width
    hessian_tile = hessian.reshape(
        hessian.shape[0], hessian.shape[1] * hessian.shape[2] * hessian.shape[3]
    )
    code_tiles = (
        codes.reshape(rows_tiles, TILE_ROWS, cols_tiles, half_width)
        .transpose(0, 2, 1, 3)
        .reshape(tile_count, pair_count)
    )
    code_onehot = (
        code_tiles[:, :, None] == lax.broadcasted_iota(jnp.int32, (1, 1, CODES), 2)
    ).astype(jnp.float32)
    book_onehot = (
        tile_map.reshape(-1)[:, None] == lax.broadcasted_iota(jnp.int32, (1, NB), 1)
    ).astype(jnp.float32)
    for iteration in range(STEPS):
        tile_books = jnp.einsum(
            "tb,bck->tck", book_onehot, codebooks, precision=lax.Precision.HIGHEST
        )
        rebuilt_tiles = jnp.einsum(
            "tpk,tck->tpc", code_onehot, tile_books, precision=lax.Precision.HIGHEST
        )
        rebuilt = (
            rebuilt_tiles.reshape(rows_tiles, cols_tiles, TILE_ROWS, half_width, 2)
            .transpose(0, 2, 1, 3, 4)
            .reshape(rows_local, cols_local)
        )
        error = rebuilt - weights.astype(jnp.float32)
        gathered = lax.all_gather(error, "col", axis=0, tiled=True)
        piece_width = cols_local // lax.axis_size("col")
        error_piece = lax.dynamic_slice_in_dim(
            gathered, lax.axis_index("col") * piece_width, piece_width, 1
        )
        error_spread = lax.all_gather(error_piece, "row", axis=1, tiled=True)
        weight_grad = 2.0 * lax.psum_scatter(
            lax.dot_general(
                error_spread,
                hessian_tile,
                (((1,), (1,)), ((), ())),
                precision=lax.Precision.HIGHEST,
                preferred_element_type=jnp.float32,
            ),
            "col",
            scatter_dimension=0,
            tiled=True,
        )
        grad_tiles = (
            weight_grad.reshape(rows_tiles, TILE_ROWS, cols_tiles, half_width, 2)
            .transpose(0, 2, 1, 3, 4)
            .reshape(tile_count, pair_count, 2)
        )
        tile_grads = jnp.einsum(
            "tpk,tpc->tck", code_onehot, grad_tiles, precision=lax.Precision.HIGHEST
        )
        local_grad = jnp.einsum(
            "tb,tck->bck", book_onehot, tile_grads, precision=lax.Precision.HIGHEST
        )
        total_even, total_odd = lax.psum((local_grad[:, 0, :], local_grad[:, 1, :]), ("row", "col"))
        book_grad = jnp.stack([total_even, total_odd], axis=1)
        codebooks = codebooks - learn_rate * book_grad
    return codebooks


def solution(mesh):
    placed = (P("row", None, "col", None), P("col", "row"), P("col", "row"), P("col", "row"), P())
    return jax.shard_map(per_device, mesh=mesh, in_specs=placed, out_specs=P(), check_vma=False)
```

profile of v0, /device:TPU:1, one launch (start us, length us, event | category | flops | bytes accessed | tf_op | source)
XLA Modules:
  0.0 803.9 jit_solution(11324388309986088203)
XLA Ops:
  8.3 1.7 fusion.16
  10.0 17.1 %fusion.3 = f32[16,2048,2]{1,2,0:T(2,128)S(1)} fusion(s32[16,2048]{1,0:T(8,128)S(1)} %bitcast_bitcast_fusion, f32[16,2,256]{2,0,1:T(8,128)S(1)} %fusion.16), kind=kOutput, calls=%fused_computation.4 | convolution fusion | flops 209715200 | bytes 425984 | tf_op jit(solution)/shard_map/tpk,tck->tpc/dot_general | solution.py:39
  27.3 1.4 copy.39
  28.7 1.1 reshape.34
  31.0 59.7 %all-gather.5.cloned.1.call-done = f32[512,2048]{1,0:T(8,128)} async-done(((f32[32,2048]{1,0:T(8,128)}), f32[512,2048]{1,0:T(8,128)}) %all-gather.5.cloned.1.call-update) | async-done | bytes 4194320 | tf_op jit(solution)/shard_map/all_gather | solution.py:48
  90.7 1.7 constant_dynamic-slice_fusion.1
  92.4 39.8 %all-gather.7.cloned.1.call-done = f32[512,1024]{1,0:T(8,128)} async-done(((f32[512,128]{1,0:T(8,128)}), f32[512,1024]{1,0:T(8,128)}) %all-gather.7.cloned.1.call-update) | async-done | bytes 2097168 | tf_op jit(solution)/shard_map/all_gather | solution.py:53
  132.2 19.4 %fusion.10 = f32[512,2048]{1,0:T(8,128)} fusion(f32[512,1024]{1,0:T(8,128)} %all-gather.7.cloned.1.call-done, f32[256,8,8,128]{3,2,1,0:T(8,128)} %bitcast.51), kind=kOutput, calls=%fused_computation.11 | convolution fusion | flops 12884901888 | bytes 14680064 | tf_op jit(solution)/shard_map/dot_general | solution.py:55
  151.8 84.1 %reduce-scatter.3.cloned.1.call-done = f32[32,2048]{1,0:T(8,128)} async-done(((f32[512,2048]{1,0:T(8,128)}), f32[32,2048]{1,0:T(8,128)}) %reduce-scatter.3.cloned.1.call-update) | async-done | bytes 262160 | tf_op jit(solution)/shard_map/reduce_scatter | solution.py:54
  235.9 1.0 broadcast_multiply_fusion.1
  237.2 1.2 reshape.36
  239.4 12.3 %fusion.2 = f32[16,2,256]{2,1,0:T(2,128)S(1)} fusion(f32[16,2048,2]{1,2,0:T(2,128)S(1)} %reshape.47, s32[16,2048]{1,0:T(8,128)} %copy-done.4), kind=kOutput, calls=%fused_computation.3 | convolution fusion | flops 209715200 | bytes 425984 | tf_op jit(solution)/shard_map/tpk,tpc->tck/dot_general | solution.py:71
  252.4 1.0 fusion.38
  253.5 148.0 %all-reduce.7.cloned.1.call-done = (f32[512,1,256]{2,0,1:T(8,128)}, f32[512,1,256]{2,0,1:T(8,128)}) async-done(((f32[512,1,256]{2,0,1:T(8,128)}, f32[512,1,256]{2,0,1:T(8,128)}), (f32[512,1,256]{2,0,1:T(8,128)}, f32[512,1,256]{2,0,1:T(8,128)})) %all-reduce.7.cloned.1.call-update) | async-done | bytes 1048592 | tf_op jit(solution)/shard_map/psum | solution.py:77
  401.6 1.7 fusion.18
  403.3 17.1 %fusion.1 = f32[16,2048,2]{1,2,0:T(2,128)S(1)} fusion(s32[16,2048]{1,0:T(8,128)S(1)} %copy-done.5, f32[16,2,256]{2,0,1:T(8,128)S(1)} %fusion.18), kind=kOutput, calls=%fused_computation.2 | convolution fusion | flops 209715200 | bytes 425984 | tf_op jit(solution)/shard_map/tpk,tck->tpc/dot_general | solution.py:39
  420.6 1.4 copy.47
  422.0 2.1 reshape.39
  424.1 1.5 copy.48
  426.4 55.1 %all-gather.9.cloned.1.call-done = f32[512,2048]{1,0:T(8,128)} async-done(((f32[32,2048]{1,0:T(8,128)}), f32[512,2048]{1,0:T(8,128)}) %all-gather.9.cloned.1.call-update) | async-done | bytes 4194320 | tf_op jit(solution)/shard_map/all_gather | solution.py:48
  481.6 1.7 constant_dynamic-slice_fusion
  483.6 39.5 %all-gather.11.cloned.1.call-done = f32[512,1024]{1,0:T(8,128)} async-done(((f32[512,128]{1,0:T(8,128)}), f32[512,1024]{1,0:T(8,128)}) %all-gather.11.cloned.1.call-update) | async-done | bytes 2097168 | tf_op jit(solution)/shard_map/all_gather | solution.py:53
  523.1 19.4 %fusion.8 = f32[512,2048]{1,0:T(8,128)} fusion(f32[512,1024]{1,0:T(8,128)} %all-gather.11.cloned.1.call-done, f32[256,8,8,128]{3,2,1,0:T(8,128)} %bitcast.52), kind=kOutput, calls=%fused_computation.9 | convolution fusion | flops 12884901888 | bytes 14680064 | tf_op jit(solution)/shard_map/dot_general | solution.py:55
  542.8 84.0 %reduce-scatter.5.cloned.1.call-done = f32[32,2048]{1,0:T(8,128)} async-done(((f32[512,2048]{1,0:T(8,128)}), f32[32,2048]{1,0:T(8,128)}) %reduce-scatter.5.cloned.1.call-update) | async-done | bytes 262160 | tf_op jit(solution)/shard_map/reduce_scatter | solution.py:54
  626.9 1.0 broadcast_multiply_fusion
  627.8 1.3 copy.49
  629.2 2.5 reshape.40
  632.7 11.3 %fusion = f32[16,2,256]{2,1,0:T(2,128)S(1)} fusion(f32[16,2048,2]{1,2,0:T(2,128)S(1)} %reshape.48, s32[16,2048]{1,0:T(8,128)S(1)} %copy-done.6), kind=kOutput, calls=%fused_computation.1 | convolution fusion | flops 209715200 | bytes 425984 | tf_op jit(solution)/shard_map/tpk,tpc->tck/dot_general | solution.py:71
  644.7 1.0 fusion.37
  645.7 148.1 %all-reduce.5.cloned.1.call-done = (f32[512,1,256]{2,0,1:T(8,128)}, f32[512,1,256]{2,0,1:T(8,128)}) async-done(((f32[512,1,256]{2,0,1:T(8,128)}, f32[512,1,256]{2,0,1:T(8,128)}), (f32[512,1,256]{2,0,1:T(8,128)}, f32[512,1,256]{2,0,1:T(8,128)})) %all-reduce.5.cloned.1.call-update) | async-done | bytes 1048592 | tf_op jit(solution)/shard_map/psum | solution.py:77
  793.9 1.4 fusion.15
  795.3 1.8 copy.53
  (45 shorter events, 8.7 us)
Async XLA Ops:
  6.5 84.1 %all-gather.5.cloned.1.call-start = ((), (), s32[]{:S(2)}) async-start(), calls=%async_computation.2 | async-start | bytes 4456448 | tf_op jit(solution)/shard_map/all_gather | solution.py:48
  8.2 1.7 copy-start.4
  10.0 20.2 %copy-start.3 = (bf16[32,2048]{1,0:T(8,128)(2,1)S(1)}, bf16[32,2048]{1,0:T(8,128)(2,1)}, u32[]{:S(2)}) copy-start(bf16[32,2048]{1,0:T(8,128)(2,1)} %param.6) | copy-start | bytes 393220
  30.9 101.3 %all-gather.7.cloned.1.call-start = ((), (), s32[]{:S(2)}) async-start(), calls=%async_computation.3 | async-start | bytes 2359296 | tf_op jit(solution)/shard_map/all_gather | solution.py:53
  92.4 143.6 %reduce-scatter.3.cloned.1.call-start = ((), (), s32[]{:S(2)}) async-start(), calls=%async_computation.4 | async-start | bytes 4456448 | tf_op jit(solution)/shard_map/reduce_scatter | solution.py:54
  151.6 250.0 %all-reduce.7.cloned.1.call-start = ((), (), s32[]{:S(2)}) async-start(), calls=%async_computation.9 | async-start | bytes 2097152 | tf_op jit(solution)/shard_map/psum | solution.py:77
  239.2 162.3 %copy-start = (f32[512,2,256]{2,1,0:T(2,128)S(1)}, f32[512,2,256]{2,1,0:T(2,128)}, u32[]{:S(2)}) copy-start(f32[512,2,256]{2,1,0:T(2,128)} %param.9) | copy-start | bytes 3145732
  239.4 163.9 %copy-start.5 = (s32[16,2048]{1,0:T(8,128)S(1)}, s32[16,2048]{1,0:T(8,128)}, u32[]{:S(2)}) copy-start(s32[16,2048]{1,0:T(8,128)} %copy-done.4) | copy-start | bytes 393220
  253.5 228.1 %all-gather.9.cloned.1.call-start = ((), (), s32[]{:S(2)}) async-start(), calls=%async_computation.5 | async-start | bytes 4456448 | tf_op jit(solution)/shard_map/all_gather | solution.py:48
  426.4 96.7 %all-gather.11.cloned.1.call-start = ((), (), s32[]{:S(2)}) async-start(), calls=%async_computation.6 | async-start | bytes 2359296 | tf_op jit(solution)/shard_map/all_gather | solution.py:53
  483.3 143.6 %reduce-scatter.5.cloned.1.call-start = ((), (), s32[]{:S(2)}) async-start(), calls=%async_computation.7 | async-start | bytes 4456448 | tf_op jit(solution)/shard_map/reduce_scatter | solution.py:54
  542.5 90.2 %copy-start.6 = (s32[16,2048]{1,0:T(8,128)S(1)}, s32[16,2048]{1,0:T(8,128)}, u32[]{:S(2)}) copy-start(s32[16,2048]{1,0:T(8,128)} %copy-done.4) | copy-start | bytes 393220
  542.5 251.3 %all-reduce.5.cloned.1.call-start = ((), (), s32[]{:S(2)}) async-start(), calls=%async_computation.8 | async-start | bytes 2097152 | tf_op jit(solution)/shard_map/psum | solution.py:77
  632.5 161.4 %copy-start.1 = (f32[512,1,256]{2,0,1:T(8,128)S(1)}, f32[512,1,256]{2,0,1:T(8,128)}, u32[]{:S(2)}) copy-start(f32[512,1,256]{2,0,1:T(8,128)} %get-tuple-element.7) | copy-start | bytes 1572868
  632.5 161.4 %copy-start.2 = (f32[512,1,256]{2,0,1:T(8,128)S(1)}, f32[512,1,256]{2,0,1:T(8,128)}, u32[]{:S(2)}) copy-start(f32[512,1,256]{2,0,1:T(8,128)} %get-tuple-element.8) | copy-start | bytes 1572868
Sparse Core Ops, SparseCore 0:
  31.0 59.5 all-gather.4
  92.5 39.6 all-gather.6
  151.7 84.1 reduce-scatter.2
  253.6 147.8 all-reduce.6
  426.5 55.0 all-gather.8
  483.4 39.6 all-gather.10
  542.6 84.1 reduce-scatter.4
  645.9 147.9 all-reduce.4
where the time goes:
time: 804 us
  waiting for transfers between devices  659 us (82%)
  matrix products  101 us (13%)
  local copies, waits for them, and re-layouts  24.4 us (3%)
  between operations  13.7 us (2%)
    psum x2, waiting for transfers between devices, per_device(): lax.psum((local_grad[:, 0, :], local_grad[:, 1, :]), ('row', 'col'))  296 us
    reduce_scatter x2, waiting for transfers between devices, per_device(): lax.psum_scatter(lax.dot_general(error_spread, hessian_tile, (((1,), (1,)...  168 us
    all_gather x2, waiting for transfers between devices, per_device(): gathered = lax.all_gather(error, 'col', axis=0, tiled=True)  115 us
    all_gather x2, waiting for transfers between devices, per_device(): error_spread = lax.all_gather(error_piece, 'row', axis=1, tiled=True)  79.3 us
    dot_general x2, matrix products, per_device(): lax.dot_general(error_spread, hessian_tile, (((1,), (1,)), ((), ())), pre...  38.8 us
    dot_general x2, matrix products, per_device(): jnp.einsum('tpk,tck->tpc', code_onehot, tile_books, precision=lax.Precisi...  34.2 us
    dot_general x2, matrix products, per_device(): jnp.einsum('tpk,tpc->tck', code_onehot, grad_tiles, precision=lax.Precisi...  23.6 us
  transfers between devices with their start and end apart: 8, of which 8 were waited for; matrix products, arithmetic and copies ran while one was open for 0% of the time, Pallas kernels for 0%

commit v1 on v0

--- a/solution.py
+++ b/solution.py
@@ -74,7 +74,9 @@
         local_grad = jnp.einsum(
             "tb,tck->bck", book_onehot, tile_grads, precision=lax.Precision.HIGHEST
         )
-        total_even, total_odd = lax.psum((local_grad[:, 0, :], local_grad[:, 1, :]), ("row", "col"))
+        total_even, total_odd = lax.psum(
+            lax.psum((local_grad[:, 0, :], local_grad[:, 1, :]), "col"), "row"
+        )
         book_grad = jnp.stack([total_even, total_odd], axis=1)
         codebooks = codebooks - learn_rate * book_grad
     return codebooks

time: 804 us -> 953 us (1.19)
  waiting for transfers between devices: 659 us -> 803 us
    psum x2 -> x4, waiting for transfers between devices: 296 us -> 434 us  [the longest x2 282 us: per_device(): lax.psum((local_grad[:, 0, :], local_grad[:, 1, :]), 'col')]
  transfers between devices with their start and end apart: 8 -> 10, of which waited for: 8 -> 10; matrix products, arithmetic and copies ran while one was open for 0% -> 0% of each run, Pallas kernels for 0% -> 0%
where the time goes in v1:
time: 953 us; the launch traced here: 948 us
  waiting for transfers between devices  803 us (84%)
  matrix products  101 us (11%)
  local copies, waits for them, and re-layouts  24.4 us (3%)
  between operations  13.7 us (1%)
    psum x2, waiting for transfers between devices, per_device(): lax.psum((local_grad[:, 0, :], local_grad[:, 1, :]), 'col')  282 us
    reduce_scatter x2, waiting for transfers between devices, per_device(): lax.psum_scatter(lax.dot_general(error_spread, hessian_tile, (((1,), (1,)...  168 us
    psum x2, waiting for transfers between devices, per_device(): lax.psum(lax.psum((local_grad[:, 0, :], local_grad[:, 1, :]), 'col'), 'row')  152 us
    all_gather x2, waiting for transfers between devices, per_device(): gathered = lax.all_gather(error, 'col', axis=0, tiled=True)  121 us
    all_gather x2, waiting for transfers between devices, per_device(): error_spread = lax.all_gather(error_piece, 'row', axis=1, tiled=True)  79.3 us
    dot_general x2, matrix products, per_device(): lax.dot_general(error_spread, hessian_tile, (((1,), (1,)), ((), ())), pre...  38.8 us
    dot_general x2, matrix products, per_device(): jnp.einsum('tpk,tck->tpc', code_onehot, tile_books, precision=lax.Precisi...  34.2 us
    dot_general x2, matrix products, per_device(): jnp.einsum('tpk,tpc->tck', code_onehot, grad_tiles, precision=lax.Precisi...  23.6 us
  transfers between devices with their start and end apart: 10, of which 10 were waited for; matrix products, arithmetic and copies ran while one was open for 0% of the time, Pallas kernels for 0%

profile of v1, /device:TPU:1, one launch (start us, length us, event | category | flops | bytes accessed | tf_op | source)
XLA Modules:
  0.0 948.0 jit_solution(13112481926760106486)
XLA Ops:
  8.3 1.7 fusion.16
  10.0 17.1 %fusion.3 = f32[16,2048,2]{1,2,0:T(2,128)S(1)} fusion(s32[16,2048]{1,0:T(8,128)S(1)} %bitcast_bitcast_fusion, f32[16,2,256]{2,0,1:T(8,128)S(1)} %fusion.16), kind=kOutput, calls=%fused_computation.4 | convolution fusion | flops 209715200 | bytes 425984 | tf_op jit(solution)/shard_map/tpk,tck->tpc/dot_general | solution.py:39
  27.3 1.4 copy.39
  28.7 1.1 reshape.34
  31.0 59.7 %all-gather.5.cloned.1.call-done = f32[512,2048]{1,0:T(8,128)} async-done(((f32[32,2048]{1,0:T(8,128)}), f32[512,2048]{1,0:T(8,128)}) %all-gather.5.cloned.1.call-update) | async-done | bytes 4194320 | tf_op jit(solution)/shard_map/all_gather | solution.py:48
  90.7 1.7 constant_dynamic-slice_fusion.1
  92.4 39.8 %all-gather.7.cloned.1.call-done = f32[512,1024]{1,0:T(8,128)} async-done(((f32[512,128]{1,0:T(8,128)}), f32[512,1024]{1,0:T(8,128)}) %all-gather.7.cloned.1.call-update) | async-done | bytes 2097168 | tf_op jit(solution)/shard_map/all_gather | solution.py:53
  132.2 19.4 %fusion.10 = f32[512,2048]{1,0:T(8,128)} fusion(f32[512,1024]{1,0:T(8,128)} %all-gather.7.cloned.1.call-done, f32[256,8,8,128]{3,2,1,0:T(8,128)} %bitcast.63), kind=kOutput, calls=%fused_computation.11 | convolution fusion | flops 12884901888 | bytes 14680064 | tf_op jit(solution)/shard_map/dot_general | solution.py:55
  151.8 84.1 %reduce-scatter.3.cloned.1.call-done = f32[32,2048]{1,0:T(8,128)} async-done(((f32[512,2048]{1,0:T(8,128)}), f32[32,2048]{1,0:T(8,128)}) %reduce-scatter.3.cloned.1.call-update) | async-done | bytes 262160 | tf_op jit(solution)/shard_map/reduce_scatter | solution.py:54
  237.2 1.2 reshape.36
  239.4 12.3 %fusion.2 = f32[16,2,256]{2,1,0:T(2,128)S(1)} fusion(f32[16,2048,2]{1,2,0:T(2,128)S(1)} %reshape.43, s32[16,2048]{1,0:T(8,128)} %copy-done.4), kind=kOutput, calls=%fused_computation.3 | convolution fusion | flops 209715200 | bytes 425984 | tf_op jit(solution)/shard_map/tpk,tpc->tck/dot_general | solution.py:71
  252.4 1.0 slice_bitcast_fusion.3
  253.5 141.0 %all-reduce.11.cloned.1.call-done = (f32[512,256]{1,0:T(8,128)}, f32[512,256]{1,0:T(8,128)}) async-done(((f32[512,256]{1,0:T(8,128)}, f32[512,256]{1,0:T(8,128)}), (f32[512,256]{1,0:T(8,128)}, f32[512,256]{1,0:T(8,128)})) %all-reduce.11.cloned.1.call-update) | async-done | bytes 1048592 | tf_op jit(solution)/shard_map/psum | solution.py:78
  394.6 76.1 %all-reduce.15.cloned.1.call-done = (f32[512,1,256]{2,0,1:T(8,128)}, f32[512,1,256]{2,0,1:T(8,128)}) async-done(((f32[512,1,256]{2,0,1:T(8,128)}, f32[512,1,256]{2,0,1:T(8,128)}), (f32[512,1,256]{2,0,1:T(8,128)}, f32[512,1,256]{2,0,1:T(8,128)})) %all-reduce.15.cloned.1.call-update) | async-done | bytes 1048592 | tf_op jit(solution)/shard_map/psum | solution.py:77
  470.7 1.7 fusion.18
  472.4 17.1 %fusion.1 = f32[16,2048,2]{1,2,0:T(2,128)S(1)} fusion(s32[16,2048]{1,0:T(8,128)S(1)} %copy-done.5, f32[16,2,256]{2,0,1:T(8,128)S(1)} %fusion.18), kind=kOutput, calls=%fused_computation.2 | convolution fusion | flops 209715200 | bytes 425984 | tf_op jit(solution)/shard_map/tpk,tck->tpc/dot_general | solution.py:39
  489.8 1.4 copy.47
  491.1 2.1 reshape.39
  493.3 1.5 copy.48
  495.6 61.0 %all-gather.9.cloned.1.call-done = f32[512,2048]{1,0:T(8,128)} async-done(((f32[32,2048]{1,0:T(8,128)}), f32[512,2048]{1,0:T(8,128)}) %all-gather.9.cloned.1.call-update) | async-done | bytes 4194320 | tf_op jit(solution)/shard_map/all_gather | solution.py:48
  556.6 1.7 constant_dynamic-slice_fusion
  558.6 39.5 %all-gather.11.cloned.1.call-done = f32[512,1024]{1,0:T(8,128)} async-done(((f32[512,128]{1,0:T(8,128)}), f32[512,1024]{1,0:T(8,128)}) %all-gather.11.cloned.1.call-update) | async-done | bytes 2097168 | tf_op jit(solution)/shard_map/all_gather | solution.py:53
  598.1 19.4 %fusion.8 = f32[512,2048]{1,0:T(8,128)} fusion(f32[512,1024]{1,0:T(8,128)} %all-gather.11.cloned.1.call-done, f32[256,8,8,128]{3,2,1,0:T(8,128)} %bitcast.64), kind=kOutput, calls=%fused_computation.9 | convolution fusion | flops 12884901888 | bytes 14680064 | tf_op jit(solution)/shard_map/dot_general | solution.py:55
  617.6 84.3 %reduce-scatter.5.cloned.1.call-done = f32[32,2048]{1,0:T(8,128)} async-done(((f32[512,2048]{1,0:T(8,128)}), f32[32,2048]{1,0:T(8,128)}) %reduce-scatter.5.cloned.1.call-update) | async-done | bytes 262160 | tf_op jit(solution)/shard_map/reduce_scatter | solution.py:54
  702.9 1.3 copy.49
  704.2 2.5 reshape.40
  707.7 11.3 %fusion = f32[16,2,256]{2,1,0:T(2,128)S(1)} fusion(f32[16,2048,2]{1,2,0:T(2,128)S(1)} %reshape.44, s32[16,2048]{1,0:T(8,128)S(1)} %copy-done.6), kind=kOutput, calls=%fused_computation.1 | convolution fusion | flops 209715200 | bytes 425984 | tf_op jit(solution)/shard_map/tpk,tpc->tck/dot_general | solution.py:71
  719.7 1.0 slice_bitcast_fusion.1
  720.8 141.0 %all-reduce.9.cloned.1.call-done = (f32[512,256]{1,0:T(8,128)}, f32[512,256]{1,0:T(8,128)}) async-done(((f32[512,256]{1,0:T(8,128)}, f32[512,256]{1,0:T(8,128)}), (f32[512,256]{1,0:T(8,128)}, f32[512,256]{1,0:T(8,128)})) %all-reduce.9.cloned.1.call-update) | async-done | bytes 1048592 | tf_op jit(solution)/shard_map/psum | solution.py:78
  861.8 76.1 %all-reduce.13.cloned.1.call-done = (f32[512,1,256]{2,0,1:T(8,128)}, f32[512,1,256]{2,0,1:T(8,128)}) async-done(((f32[512,1,256]{2,0,1:T(8,128)}, f32[512,1,256]{2,0,1:T(8,128)}), (f32[512,1,256]{2,0,1:T(8,128)}, f32[512,1,256]{2,0,1:T(8,128)})) %all-reduce.13.cloned.1.call-update) | async-done | bytes 1048592 | tf_op jit(solution)/shard_map/psum | solution.py:77
  937.9 1.4 fusion.15
  939.4 1.8 copy.53
  (51 shorter events, 10.4 us)
Async XLA Ops:
  6.5 84.1 %all-gather.5.cloned.1.call-start = ((), (), s32[]{:S(2)}) async-start(), calls=%async_computation.2 | async-start | bytes 4456448 | tf_op jit(solution)/shard_map/all_gather | solution.py:48
  8.2 1.7 copy-start.4
  10.0 20.2 %copy-start.3 = (bf16[32,2048]{1,0:T(8,128)(2,1)S(1)}, bf16[32,2048]{1,0:T(8,128)(2,1)}, u32[]{:S(2)}) copy-start(bf16[32,2048]{1,0:T(8,128)(2,1)} %param.6) | copy-start | bytes 393220
  30.9 101.3 %all-gather.7.cloned.1.call-start = ((), (), s32[]{:S(2)}) async-start(), calls=%async_computation.3 | async-start | bytes 2359296 | tf_op jit(solution)/shard_map/all_gather | solution.py:53
  92.4 143.6 %reduce-scatter.3.cloned.1.call-start = ((), (), s32[]{:S(2)}) async-start(), calls=%async_computation.4 | async-start | bytes 4456448 | tf_op jit(solution)/shard_map/reduce_scatter | solution.py:54
  151.6 242.9 %all-reduce.11.cloned.1.call-start = ((), (), s32[]{:S(2)}) async-start(), calls=%async_computation.9 | async-start | bytes 2097152 | tf_op jit(solution)/shard_map/psum | solution.py:78
  239.2 231.5 %copy-start = (f32[512,2,256]{2,1,0:T(2,128)S(1)}, f32[512,2,256]{2,1,0:T(2,128)}, u32[]{:S(2)}) copy-start(f32[512,2,256]{2,1,0:T(2,128)} %param.9) | copy-start | bytes 3145732
  239.4 233.0 %copy-start.5 = (s32[16,2048]{1,0:T(8,128)S(1)}, s32[16,2048]{1,0:T(8,128)}, u32[]{:S(2)}) copy-start(s32[16,2048]{1,0:T(8,128)} %copy-done.4) | copy-start | bytes 393220
  253.5 217.2 %all-reduce.15.cloned.1.call-start = ((), (), s32[]{:S(2)}) async-start(), calls=%async_computation.11 | async-start | bytes 2097152 | tf_op jit(solution)/shard_map/psum | solution.py:77
  394.6 162.0 %all-gather.9.cloned.1.call-start = ((), (), s32[]{:S(2)}) async-start(), calls=%async_computation.5 | async-start | bytes 4456448 | tf_op jit(solution)/shard_map/all_gather | solution.py:48
  495.5 102.6 %all-gather.11.cloned.1.call-start = ((), (), s32[]{:S(2)}) async-start(), calls=%async_computation.6 | async-start | bytes 2359296 | tf_op jit(solution)/shard_map/all_gather | solution.py:53
  558.3 143.6 %reduce-scatter.5.cloned.1.call-start = ((), (), s32[]{:S(2)}) async-start(), calls=%async_computation.7 | async-start | bytes 4456448 | tf_op jit(solution)/shard_map/reduce_scatter | solution.py:54
  617.5 90.2 %copy-start.6 = (s32[16,2048]{1,0:T(8,128)S(1)}, s32[16,2048]{1,0:T(8,128)}, u32[]{:S(2)}) copy-start(s32[16,2048]{1,0:T(8,128)} %copy-done.4) | copy-start | bytes 393220
  617.5 244.2 %all-reduce.9.cloned.1.call-start = ((), (), s32[]{:S(2)}) async-start(), calls=%async_computation.8 | async-start | bytes 2097152 | tf_op jit(solution)/shard_map/psum | solution.py:78
  707.5 230.4 %copy-start.1 = (f32[512,1,256]{2,0,1:T(8,128)S(1)}, f32[512,1,256]{2,0,1:T(8,128)}, u32[]{:S(2)}) copy-start(f32[512,1,256]{2,0,1:T(8,128)} %get-tuple-element.11) | copy-start | bytes 1572868
  707.5 230.4 %copy-start.2 = (f32[512,1,256]{2,0,1:T(8,128)S(1)}, f32[512,1,256]{2,0,1:T(8,128)}, u32[]{:S(2)}) copy-start(f32[512,1,256]{2,0,1:T(8,128)} %get-tuple-element.12) | copy-start | bytes 1572868
  720.8 217.2 %all-reduce.13.cloned.1.call-start = ((), (), s32[]{:S(2)}) async-start(), calls=%async_computation.10 | async-start | bytes 2097152 | tf_op jit(solution)/shard_map/psum | solution.py:77
Sparse Core Ops, SparseCore 0:
  31.0 59.5 all-gather.4
  92.5 39.6 all-gather.6
  151.7 84.1 reduce-scatter.2
  253.6 140.8 all-reduce.10
  396.9 73.7 all-reduce.14
  495.7 60.8 all-gather.8
  558.4 39.6 all-gather.10
  617.6 84.1 reduce-scatter.4
  720.9 140.8 all-reduce.8
  864.2 73.7 all-reduce.12
